TPU v7x, 32 devices: a whole 2x2x4 slice. The times are simulated.
32 devices in a mesh: tok: 8 (over z, y), wid: 4 (over x, core).
Axes of the slice: x: 2, y: 2, z: 4, core: 2. Of those that a mesh axis runs over, the one named last changes fastest.
Arguments:
- queries: bfloat16 [1024, 8192], P('tok', 'wid'), may hold values from -6 to 6
- key_branch: bfloat16 [1024, 8192], P('tok', 'wid'), may hold values from -6 to 6
- value_branch: bfloat16 [1024, 8192], P('tok', 'wid'), may hold values from -6 to 6
- filters: float32 [512, 128], P('wid'), may hold values from -0.5 to 0.5
- out_weight: bfloat16 [8192, 8192], P(None, 'wid'), may hold values from -0.09375 to 0.09375
- cotangent: bfloat16 [1024, 8192], P('tok', 'wid'), may hold values from -6 to 6
Outputs:
- layer_out: bfloat16 [1024, 8192], P('tok', 'wid')
- grad_queries: bfloat16 [1024, 8192], P('tok', 'wid')
- grad_keys: bfloat16 [1024, 8192], P('tok', 'wid')
- grad_values: bfloat16 [1024, 8192], P('tok', 'wid')
- grad_filters: float32 [512, 128], P('wid')
All inputs are finite; a program needn't handle non-finite values.
Results may differ from a plain program's by a relative error of at most 0.02.
Values may be sent and summed in bfloat16 or wider, within the bound.
A program may use at most 192 MiB of HBM per device.

v0:
```python
import math
import jax
import jax.numpy as jnp
from jax import lax
from jax.sharding import PartitionSpec as P


def shifted(block, axis, distance):
    devices = range(lax.axis_size(axis))
    route = [(i - distance, i) for i in devices if i - distance in devices]
    return lax.ppermute(block, axis, route)


def causal_matrix(filters):
    groups, kernel = filters.shape
    span = 2 * kernel
    reverse = filters[:, ::-1]
    padded = jnp.concatenate(
        [
            jnp.zeros((groups, 1), jnp.float32),
            reverse,
            jnp.zeros((groups, span - kernel), jnp.float32),
        ],
        axis=1,
    )
    tiled = jnp.tile(padded, (1, kernel))[:, : kernel * span]
    return tiled.reshape(groups, kernel, span)


def split_pair(matrix):
    upper = matrix.astype(jnp.bfloat16)
    lower = (matrix - upper.astype(jnp.float32)).astype(jnp.bfloat16)
    return (upper, lower)


def split_einsum(form, pair, data):
    first = jnp.einsum(form, pair[0], data, preferred_element_type=jnp.float32)
    second = jnp.einsum(form, pair[1], data, preferred_element_type=jnp.float32)
    return first + second


def block_windows(extended, kernel, groups, group_size):
    blocks = extended.reshape(extended.shape[0] // kernel, kernel, groups, group_size)
    return jnp.concatenate([blocks[:-1], blocks[1:]], axis=1)


def gated_gradient(cotangent, out_weight):
    return (
        lax.psum_scatter(
            lax.dot_general(
                out_weight, cotangent, (((1,), (1,)), ((), ())), preferred_element_type=jnp.float32
            ).astype(jnp.bfloat16),
            "wid",
            scatter_dimension=0,
            tiled=True,
        )
        .astype(jnp.float32)
        .T
    )


def local(queries, key_branch, value_branch, filters, out_weight, cotangent):
    length, width = queries.shape
    groups, kernel = filters.shape
    group_size = width // groups
    nblocks = length // kernel
    kv = (key_branch.astype(jnp.float32) * value_branch.astype(jnp.float32)).astype(jnp.bfloat16)
    rim = shifted(kv, "tok", 1)
    extended = jnp.concatenate([rim, kv], axis=0)
    windows = block_windows(extended, kernel, groups, group_size)
    toeplitz = split_pair(causal_matrix(filters))
    conv = split_einsum("gts,bsgc->btgc", toeplitz, windows).reshape(length, width)
    gated = (queries.astype(jnp.float32) * conv).astype(jnp.bfloat16)
    layer_out = jnp.dot(
        lax.all_gather(gated, "wid", axis=1, tiled=True),
        out_weight,
        preferred_element_type=jnp.float32,
    ).astype(jnp.bfloat16)
    grad_gated = gated_gradient(cotangent, out_weight)
    grad_conv = (grad_gated * queries.astype(jnp.float32)).astype(jnp.bfloat16)
    grad_queries = (grad_gated * conv).astype(jnp.bfloat16)
    grad_blocks = grad_conv.reshape(nblocks, kernel, groups, group_size)
    spread = split_einsum("gts,btgc->bsgc", toeplitz, grad_blocks)
    lower_half = spread[:, :kernel]
    upper_half = spread[:, kernel:]
    returned = shifted(lower_half[0].reshape(kernel, width).astype(jnp.bfloat16), "tok", -1).astype(
        jnp.float32
    )
    tail = jnp.concatenate(
        [lower_half[1:], returned.reshape(1, kernel, groups, group_size)], axis=0
    )
    grad_kv = (upper_half + tail).reshape(length, width)
    grad_keys = (grad_kv * value_branch.astype(jnp.float32)).astype(jnp.bfloat16)
    grad_values = (grad_kv * key_branch.astype(jnp.float32)).astype(jnp.bfloat16)
    products = jnp.einsum(
        "btgc,bsgc->gts", grad_blocks, windows, preferred_element_type=jnp.float32
    )
    flat = jnp.pad(products.reshape(groups, kernel * 2 * kernel), ((0, 0), (0, kernel)))
    skewed = flat.reshape(groups, kernel, 2 * kernel + 1).sum(axis=1)
    local_terms = skewed[:, 1 : kernel + 1][:, ::-1]
    summed = lax.psum(local_terms, "tok")
    scale_factor = 1.0 / math.sqrt(length * lax.axis_size("tok") * group_size)
    grad_filters = summed * scale_factor
    return (layer_out, grad_queries, grad_keys, grad_values, grad_filters)


def solution(mesh):
    return jax.shard_map(
        local,
        mesh=mesh,
        in_specs=(
            P("tok", "wid"),
            P("tok", "wid"),
            P("tok", "wid"),
            P("wid", None),
            P(None, "wid"),
            P("tok", "wid"),
        ),
        out_specs=(
            P("tok", "wid"),
            P("tok", "wid"),
            P("tok", "wid"),
            P("tok", "wid"),
            P("wid", None),
        ),
        check_vma=False,
    )
```

profile of v0, /device:TPU:0, one launch (start us, length us, event | category | flops | bytes accessed | tf_op | source)
XLA Modules:
  0.0 323.4 jit_solution(6530451499667047419)
XLA Ops:
  7.2 1.0 copy-done
  8.2 16.6 %convolution_convert_fusion = bf16[8192,128]{1,0:T(8,128)(2,1)} fusion(bf16[8192,2048]{1,0:T(8,128)(2,1)} %param.10, bf16[128,2048]{1,0:T(8,128)(2,1)S(1)} %copy-done), kind=kOutput, calls=%fused_computation.1 | convolution fusion | flops 4296015872 | bytes 36175872 | tf_op jit(solution)/shard_map/dot_general | solution.py:50
  25.6 7.1 %tile.4 = f32[128,128,257]{0,2,1:T(8,128)} broadcast(f32[128,257]{0,1:T(8,128)S(1)} %copy.29), dimensions={0,2} | broadcast | bytes 16974336 | tf_op jit(solution)/shard_map/tile | solution.py:26
  32.7 17.8 %tile.10 = f32[128,32896]{0,1:T(8,128)} reshape(f32[128,128,257]{0,2,1:T(8,128)} %tile.4) | data formatting | bytes 33685504 | tf_op jit(solution)/shard_map/tile | solution.py:26
  50.5 11.4 %slice.27 = f32[128,32768]{0,1:T(8,128)} slice(f32[128,32896]{0,1:T(8,128)} %tile.10), slice={[0:128], [0:32768]} | slice | bytes 33554432 | tf_op jit(solution)/shard_map/slice | solution.py:26
  61.9 17.7 %copy.36 = f32[128,128,256]{2,1,0:T(8,128)} copy(f32[128,128,256]{0,2,1:T(8,128)} %bitcast.44) | data formatting | bytes 33554432 | tf_op jit(solution)/shard_map/reshape | solution.py:27
  79.6 1.2 fusion.1
  80.8 7.2 %fusion.11 = f32[128,16,256]{2,1,0:T(8,128)S(1)} fusion(bf16[128,128,16]{0,2,1:T(8,128)(2,1)S(1)} %bitcast.52, f32[128,128,256]{2,1,0:T(8,128)} %copy.36), kind=kOutput, calls=%fused_computation.27 | convolution fusion | flops 138412032 | bytes 19398656 | tf_op jit(solution)/shard_map/gts,btgc->bsgc/dot_general | solution.py:37
  88.0 3.5 %copy-done.2 = f32[128,128,256]{2,1,0:T(8,128)S(1)} copy-done((f32[128,128,256]{2,1,0:T(8,128)S(1)}, f32[128,128,256]{2,1,0:T(8,128)}, u32[]{:S(2)}) %copy-start.2) | copy-done | bytes 16777240
  91.5 1.2 add_bitcast_fusion
  92.8 1.3 collective-permute-start.1
  94.1 15.5 %collective-permute-done.1 = bf16[128,2048]{0,1:T(8,128)(2,1)S(1)} collective-permute-done((bf16[128,2048]{0,1:T(8,128)(2,1)S(1)}, bf16[128,2048]{0,1:T(8,128)(2,1)S(1)}, u32[]{:S(2)}, u32[]{:S(2)}) %collective-permute-start.1) | collective-permute-done | bytes 524320 | tf_op jit(solution)/shard_map/ppermute | solution.py:11
  109.8 0.3 copy.31
  110.1 2.4 fusion.2
  112.5 4.7 %collective-permute-start = (bf16[128,2048]{1,0:T(8,128)(2,1)S(1)}, bf16[128,2048]{1,0:T(8,128)(2,1)S(1)}, u32[]{:S(2)}, u32[]{:S(2)}) collective-permute-start(bf16[128,2048]{1,0:T(8,128)(2,1)S(1)} %get-tuple-element.22), channel_id=1, source_target_pairs={{0,4},{4,8},{8,12},{12,16},{16,20},{20,24},{24,28},{1,5},{5,9},{9,... | collective-permute-start | bytes 1572872 | tf_op jit(solution)/shard_map/ppermute | solution.py:11
  117.5 9.7 %collective-permute-done = bf16[128,2048]{1,0:T(8,128)(2,1)S(1)} collective-permute-done((bf16[128,2048]{1,0:T(8,128)(2,1)S(1)}, bf16[128,2048]{1,0:T(8,128)(2,1)S(1)}, u32[]{:S(2)}, u32[]{:S(2)}) %collective-permute-start) | collective-permute-done | bytes 524320 | tf_op jit(solution)/shard_map/ppermute | solution.py:11
  127.2 0.3 copy.27
  127.5 9.2 %fusion.7 = f32[128,16,128]{2,1,0:T(8,128)} fusion(bf16[1,128,128,16]{1,3,2,0:T(8,128)(2,1)S(1)} %bitcast.46, bf16[1,128,128,16]{1,3,2,0:T(8,128)(2,1)S(1)} %bitcast.49, f32[128,128,256]{2,1,0:T(8,128)} %copy.36), kind=kOutput, calls=%fused_computation.21 | convolution fusion | flops 140509184 | bytes 18874368 | tf_op jit(solution)/shard_map/gts,bsgc->btgc/dot_general | solution.py:37
  136.8 8.2 %fusion.6 = f32[128,128,256]{2,1,0:T(8,128)} fusion(bf16[128,128,16]{0,2,1:T(8,128)(2,1)S(1)} %bitcast.54, bf16[1,128,128,16]{1,3,2,0:T(8,128)(2,1)S(1)} %bitcast.47, bf16[1,128,128,16]{1,3,2,0:T(8,128)(2,1)S(1)} %bitcast.50), kind=kOutput, calls=%fused_computation.20 | convolution fusion | flops 136314880 | bytes 18350080 | tf_op jit(solution)/shard_map/btgc,bsgc->gts/dot_general | solution.py:95
  145.0 4.5 %convolution_add_fusion = f32[128,16,128]{2,1,0:T(8,128)} fusion(f32[128,16,128]{2,1,0:T(8,128)} %fusion.7, bf16[1,128,128,16]{1,3,2,0:T(8,128)(2,1)S(1)} %bitcast.48, bf16[1,128,128,16]{1,3,2,0:T(8,128)(2,1)S(1)} %bitcast.51, f32[128,128,256]{2,1,0:T(8,128)S(1)} %bitcast.43), kind=kOutput, calls=%fused_computation.4 | convolution fusion | flops 153354240 | bytes 19922944 | tf_op jit(solution)/shard_map/gts,bsgc->btgc/dot_general | solution.py:38
  149.5 17.9 %copy.37 = f32[128,128,256]{0,2,1:T(8,128)} copy(f32[128,128,256]{2,1,0:T(8,128)} %fusion.6) | data formatting | bytes 33554432 | tf_op jit(solution)/shard_map/reshape | solution.py:98
  167.4 13.3 %pad.4 = f32[128,32896]{0,1:T(8,128)} pad(f32[128,32768]{0,1:T(8,128)} %bitcast.45, f32[]{:T(128)} %constant.2.clone.1), padding=0_0x0_128 | pad | bytes 33619972 | tf_op jit(solution)/shard_map/jit(_pad)/pad | solution.py:98
  180.7 17.5 %reshape.67 = f32[128,128,257]{0,2,1:T(8,128)} reshape(f32[128,32896]{0,1:T(8,128)} %pad.4) | data formatting | bytes 33685504 | tf_op jit(solution)/shard_map/reshape | solution.py:99
  198.2 6.9 %reduce_sum.9 = f32[128,257]{0,1:T(8,128)S(1)} reduce(f32[128,128,257]{0,2,1:T(8,128)} %reshape.67, f32[]{:T(128)} %constant.2.clone.1), dimensions={1}, to_apply=%region_1.2 | reduce | flops 4177792 | bytes 16974340 | tf_op jit(solution)/shard_map/reduce_sum | solution.py:99
  205.0 0.6 rev.7
  206.0 1.0 fusion.5
  207.0 1.0 copy.34
  208.0 67.5 %all-reduce.3.cloned.1.call-done = f32[128,128]{0,1:T(8,128)} async-done(((f32[128,128]{0,1:T(8,128)}), f32[128,128]{0,1:T(8,128)}) %all-reduce.3.cloned.1.call-update) | async-done | bytes 65552 | tf_op jit(solution)/shard_map/psum | solution.py:101
  275.6 0.8 broadcast_multiply_fusion
  276.4 0.7 copy.35
  277.1 23.2 %all-gather.2.cloned.1.call-done = bf16[128,8192]{0,1:T(8,128)(2,1)} async-done(((bf16[128,2048]{0,1:T(8,128)(2,1)}), bf16[128,8192]{0,1:T(8,128)(2,1)}) %all-gather.2.cloned.1.call-update) | async-done | bytes 2097168 | tf_op jit(solution)/shard_map/all_gather | solution.py:75
  300.4 16.5 %convolution_convert_fusion.1 = bf16[128,2048]{1,0:T(8,128)(2,1)} fusion(bf16[128,8192]{0,1:T(8,128)(2,1)} %all-gather.2.cloned.1.call-done, bf16[8192,2048]{1,0:T(8,128)(2,1)} %param.10), kind=kOutput, calls=%fused_computation.2 | convolution fusion | flops 4295229440 | bytes 36175872 | tf_op jit(solution)/shard_map/dot_general | solution.py:74
  (49 shorter events, 1.7 us)
Async XLA Ops:
  7.2 1.1 copy-start
  7.2 17.8 %copy-start.11 = (f32[128,128]{1,0:T(8,128)S(1)}, f32[128,128]{1,0:T(8,128)}, u32[]{:S(2)}) copy-start(f32[128,128]{1,0:T(8,128)} %param.9) | copy-start | bytes 196612
  7.2 18.1 %copy-start.10 = (bf16[128,2048]{1,0:T(8,128)(2,1)S(1)}, bf16[128,2048]{1,0:T(8,128)(2,1)}, u32[]{:S(2)}) copy-start(bf16[128,2048]{1,0:T(8,128)(2,1)} %param.6) | copy-start | bytes 1572868
  7.2 72.4 %reduce-scatter.2.cloned.1.call-start = ((), (), s32[]{:S(2)}) async-start(), calls=%async_computation.2 | async-start | bytes 2621440 | tf_op jit(solution)/shard_map/reduce_scatter | solution.py:49
  24.9 250.7 %all-reduce.3.cloned.1.call-start = ((), (), s32[]{:S(2)}) async-start(), calls=%async_computation.3 | async-start | bytes 131072 | tf_op jit(solution)/shard_map/psum | solution.py:101
  25.6 54.0 %copy-start.5 = (bf16[128,2048]{0,1:T(8,128)(2,1)}, bf16[128,2048]{0,1:T(8,128)(2,1)S(1)}, u32[]{:S(2)}) copy-start(bf16[128,2048]{0,1:T(8,128)(2,1)S(1)} %copy.26) | copy-start | bytes 1572868
  80.7 7.2 %copy-start.3 = (bf16[128,2048]{0,1:T(8,128)(2,1)}, bf16[128,2048]{0,1:T(8,128)(2,1)S(1)}, u32[]{:S(2)}) copy-start(bf16[128,2048]{0,1:T(8,128)(2,1)S(1)} %fusion.1) | copy-start | bytes 1572868
  80.8 10.7 %copy-start.2 = (f32[128,128,256]{2,1,0:T(8,128)S(1)}, f32[128,128,256]{2,1,0:T(8,128)}, u32[]{:S(2)}) copy-start(f32[128,128,256]{2,1,0:T(8,128)} %copy.36) | copy-start | bytes 50331652
  91.5 18.6 %copy-start.9 = (bf16[128,2048]{1,0:T(8,128)(2,1)S(1)}, bf16[128,2048]{1,0:T(8,128)(2,1)}, u32[]{:S(2)}) copy-start(bf16[128,2048]{1,0:T(8,128)(2,1)} %param.7) | copy-start | bytes 1572868
  92.8 16.8 %collective-permute-start.1 = (bf16[128,2048]{0,1:T(8,128)(2,1)S(1)}, bf16[128,2048]{0,1:T(8,128)(2,1)S(1)}, u32[]{:S(2)}, u32[]{:S(2)}) collective-permute-start(bf16[128,2048]{0,1:T(8,128)(2,1)S(1)} %bitcast.57), channel_id=1, source_target_pairs={{4,0},{8,4},{12,8},{16,12},{20,16},{24,20},{28,24},{5,1},{9,5},{13... | collective-permute-start | bytes 1572872 | tf_op jit(solution)/shard_map/ppermute | solution.py:11
  112.5 14.7 %collective-permute-start = (bf16[128,2048]{1,0:T(8,128)(2,1)S(1)}, bf16[128,2048]{1,0:T(8,128)(2,1)S(1)}, u32[]{:S(2)}, u32[]{:S(2)}) collective-permute-start(bf16[128,2048]{1,0:T(8,128)(2,1)S(1)} %get-tuple-element.22), channel_id=1, source_target_pairs={{0,4},{4,8},{8,12},{12,16},{16,20},{20,24},{24,28},{1,5},{5,9},{9,... | collective-permute-start | bytes 1572872 | tf_op jit(solution)/shard_map/ppermute | solution.py:11
  127.5 9.3 %copy-start.4 = (bf16[128,2048]{0,1:T(8,128)(2,1)S(1)}, bf16[128,2048]{0,1:T(8,128)(2,1)}, u32[]{:S(2)}) copy-start(bf16[128,2048]{0,1:T(8,128)(2,1)} %copy-done.3) | copy-start | bytes 1572868
  127.5 17.4 %slice-start = ((s8[16777216]{0:T(1024)(128)(4,1)}), s8[4194304]{0:T(1024)(128)(4,1)S(1)}, s32[]{:S(2)}) async-start(s8[16777216]{0:T(1024)(128)(4,1)} %bitcast.42), calls=%async_computation.4 | async-start | bytes 8388608
  127.5 17.4 %slice-start.1 = ((s8[16777216]{0:T(1024)(128)(4,1)}), s8[4194304]{0:T(1024)(128)(4,1)S(1)}, s32[]{:S(2)}) async-start(s8[16777216]{0:T(1024)(128)(4,1)} %bitcast.42), calls=%async_computation.5 | async-start | bytes 8388608
  127.5 17.4 %slice-start.2 = ((s8[16777216]{0:T(1024)(128)(4,1)}), s8[4194304]{0:T(1024)(128)(4,1)S(1)}, s32[]{:S(2)}) async-start(s8[16777216]{0:T(1024)(128)(4,1)} %bitcast.42), calls=%async_computation.6 | async-start | bytes 8388608
  136.8 8.2 %slice-start.3 = ((s8[16777216]{0:T(1024)(128)(4,1)}), s8[4194304]{0:T(1024)(128)(4,1)S(1)}, s32[]{:S(2)}) async-start(s8[16777216]{0:T(1024)(128)(4,1)} %bitcast.42), calls=%async_computation.7 | async-start | bytes 8388608
  198.1 7.8 %copy-start.6 = (bf16[128,2048]{0,1:T(8,128)(2,1)S(1)}, bf16[128,2048]{0,1:T(8,128)(2,1)}, u32[]{:S(2)}) copy-start(bf16[128,2048]{0,1:T(8,128)(2,1)} %copy-done.5) | copy-start | bytes 1572868
  198.1 7.8 %copy-start.7 = (f32[128,16,128]{2,1,0:T(8,128)S(1)}, f32[128,16,128]{2,1,0:T(8,128)}, u32[]{:S(2)}) copy-start(f32[128,16,128]{2,1,0:T(8,128)} %convolution_add_fusion) | copy-start | bytes 3145732
  198.2 7.8 %copy-start.8 = (bf16[2048,128]{1,0:T(8,128)(2,1)S(1)}, bf16[2048,128]{1,0:T(8,128)(2,1)}, u32[]{:S(2)}) copy-start(bf16[2048,128]{1,0:T(8,128)(2,1)} %reduce-scatter.2.cloned.1.call-done) | copy-start | bytes 1572868
  205.7 94.6 %all-gather.2.cloned.1.call-start = ((), (), s32[]{:S(2)}) async-start(), calls=%async_computation.1 | async-start | bytes 2621440 | tf_op jit(solution)/shard_map/all_gather | solution.py:75
  300.3 16.5 %copy-start.1 = (bf16[128,2048]{1,0:T(8,128)(2,1)S(1)}, bf16[128,2048]{1,0:T(8,128)(2,1)}, u32[]{:S(2)}) copy-start(bf16[128,2048]{1,0:T(8,128)(2,1)} %param.11) | copy-start | bytes 1572868
Sparse Core Ops, SparseCore 0:
  25.0 34.1 reduce-scatter.1
  205.8 69.7 all-reduce.2
  277.8 22.5 all-gather.1
where the time goes:
time: 325 us; the launch traced here: 323 us
  waiting for transfers between devices  116 us (36%)
  local copies, waits for them, and re-layouts  111 us (34%)
  matrix products  63.5 us (20%)
  between operations  14 us (4%)
  other arithmetic  12.5 us (4%)
  starting transfers between devices  6.37 us (2%)
    psum x1, waiting for transfers between devices, local(): summed = lax.psum(local_terms, 'tok')  67.5 us
    ppermute x2, waiting for transfers between devices, shifted(): return lax.ppermute(block, axis, route)  25.2 us
    another operation x2, local copies, waits for them, and re-layouts, causal_matrix(): tiled = jnp.tile(padded, (1, kernel))[:, :kernel * span]  24.9 us
    all_gather x1, waiting for transfers between devices, local(): lax.all_gather(gated, 'wid', axis=1, tiled=True)  23.2 us
    reshape x1, local copies, waits for them, and re-layouts, local(): products.reshape(groups, kernel * 2 * kernel)  17.9 us
    reshape x1, local copies, waits for them, and re-layouts, causal_matrix(): return tiled.reshape(groups, kernel, span)  17.7 us
    reshape x1, local copies, waits for them, and re-layouts, local(): skewed = flat.reshape(groups, kernel, 2 * kernel + 1).sum(axis=1)  17.5 us
    dot_general x1, matrix products, gated_gradient(): lax.dot_general(out_weight, cotangent, (((1,), (1,)), ((), ())), preferre...  16.6 us
  transfers between devices with their start and end apart: 5, of which 4 were waited for; matrix products, arithmetic and copies ran while one was open for 18% of the time, Pallas kernels for 0%

commit v1 on v0

--- a/solution.py
+++ b/solution.py
@@ -98,7 +98,8 @@
     flat = jnp.pad(products.reshape(groups, kernel * 2 * kernel), ((0, 0), (0, kernel)))
     skewed = flat.reshape(groups, kernel, 2 * kernel + 1).sum(axis=1)
     local_terms = skewed[:, 1 : kernel + 1][:, ::-1]
-    summed = lax.psum(local_terms, "tok")
+    parts = lax.all_gather(local_terms, "tok")
+    summed = jnp.sum(parts, axis=0)
     scale_factor = 1.0 / math.sqrt(length * lax.axis_size("tok") * group_size)
     grad_filters = summed * scale_factor
     return (layer_out, grad_queries, grad_keys, grad_values, grad_filters)

time: 325 us -> 276 us (0.85)
  waiting for transfers between devices: 116 us -> 25.2 us
  blocking collectives: 0 us -> 33 us
  matrix products: 63.5 us -> 71.1 us
    psum x1 -> x0, waiting for transfers between devices: 67.5 us -> none  [local(): summed = lax.psum(local_terms, 'tok')]
    all_gather x0 -> x1, blocking collectives: none -> 33 us  [local(): parts = lax.all_gather(local_terms, 'tok')]
    all_gather x1, waiting for transfers between devices: 23.2 us -> 0.01 us  [local(): lax.all_gather(gated, 'wid', axis=1, tiled=True)]
    dot_general x2, matrix products: 5.75 us -> 14.1 us  [split_einsum(): second = jnp.einsum(form, pair[1], data, preferred_element_type=jnp.float32)]
    unnamed x35 -> x18, local copies, waits for them, and re-layouts: 6.57 us -> 6.51 us
  transfers between devices with their start and end apart: 5 -> 4, of which waited for: 4 -> 2; matrix products, arithmetic and copies ran while one was open for 18% -> 44% of each run, Pallas kernels for 0% -> 0%
where the time goes in v1:
time: 276 us; the launch traced here: 274 us
  local copies, waits for them, and re-layouts  112 us (41%)
  matrix products  71.1 us (26%)
  blocking collectives  33 us (12%)
  waiting for transfers between devices  25.2 us (9%)
  between operations  14.2 us (5%)
  other arithmetic  12.7 us (5%)
  starting transfers between devices  6.11 us (2%)
    all_gather x1, blocking collectives, local(): parts = lax.all_gather(local_terms, 'tok')  33 us
    ppermute x2, waiting for transfers between devices, shifted(): return lax.ppermute(block, axis, route)  25.2 us
    another operation x2, local copies, waits for them, and re-layouts, causal_matrix(): tiled = jnp.tile(padded, (1, kernel))[:, :kernel * span]  24.9 us
    reshape x1, local copies, waits for them, and re-layouts, local(): products.reshape(groups, kernel * 2 * kernel)  17.9 us
    reshape x1, local copies, waits for them, and re-layouts, causal_matrix(): return tiled.reshape(groups, kernel, span)  17.7 us
    reshape x1, local copies, waits for them, and re-layouts, local(): skewed = flat.reshape(groups, kernel, 2 * kernel + 1).sum(axis=1)  17.5 us
    dot_general x1, matrix products, gated_gradient(): lax.dot_general(out_weight, cotangent, (((1,), (1,)), ((), ())), preferre...  16.6 us
    dot_general x1, matrix products, local(): jnp.dot(lax.all_gather(gated, 'wid', axis=1, tiled=True), out_weight, pre...  16.5 us
  transfers between devices with their start and end apart: 4, of which 2 were waited for; matrix products, arithmetic and copies ran while one was open for 44% of the time, Pallas kernels for 0%

profile of v1, /device:TPU:0, one launch (start us, length us, event | category | flops | bytes accessed | tf_op | source)
XLA Modules:
  0.0 273.9 jit_solution(13379779544495700143)
XLA Ops:
  7.2 1.0 copy-done
  8.2 16.6 %convolution_convert_fusion = bf16[8192,128]{1,0:T(8,128)(2,1)} fusion(bf16[8192,2048]{1,0:T(8,128)(2,1)} %param.10, bf16[128,2048]{1,0:T(8,128)(2,1)S(1)} %copy-done), kind=kOutput, calls=%fused_computation.1 | convolution fusion | flops 4296015872 | bytes 36175872 | tf_op jit(solution)/shard_map/dot_general | solution.py:50
  25.3 0.3 copy.35
  25.6 7.1 %tile.4 = f32[128,128,257]{0,2,1:T(8,128)} broadcast(f32[128,257]{0,1:T(8,128)S(1)} %copy.38), dimensions={0,2} | broadcast | bytes 16974336 | tf_op jit(solution)/shard_map/tile | solution.py:26
  32.7 17.8 %tile.10 = f32[128,32896]{0,1:T(8,128)} reshape(f32[128,128,257]{0,2,1:T(8,128)} %tile.4) | data formatting | bytes 33685504 | tf_op jit(solution)/shard_map/tile | solution.py:26
  50.5 11.4 %slice.27 = f32[128,32768]{0,1:T(8,128)} slice(f32[128,32896]{0,1:T(8,128)} %tile.10), slice={[0:128], [0:32768]} | slice | bytes 33554432 | tf_op jit(solution)/shard_map/slice | solution.py:26
  61.9 17.7 %copy.45 = f32[128,128,256]{2,1,0:T(8,128)} copy(f32[128,128,256]{0,2,1:T(8,128)} %bitcast.47) | data formatting | bytes 33554432 | tf_op jit(solution)/shard_map/reshape | solution.py:27
  79.6 1.2 fusion.1
  80.7 7.1 %fusion.11 = f32[128,16,256]{2,1,0:T(8,128)S(1)} fusion(bf16[128,128,16]{0,2,1:T(8,128)(2,1)S(1)} %bitcast.55, f32[128,128,256]{2,1,0:T(8,128)} %copy.45), kind=kOutput, calls=%fused_computation.28 | convolution fusion | flops 138412032 | bytes 19398656 | tf_op jit(solution)/shard_map/gts,btgc->bsgc/dot_general | solution.py:37
  87.9 3.4 %copy-done.2 = f32[128,128,256]{2,1,0:T(8,128)S(1)} copy-done((f32[128,128,256]{2,1,0:T(8,128)S(1)}, f32[128,128,256]{2,1,0:T(8,128)}, u32[]{:S(2)}) %copy-start.2) | copy-done | bytes 16777240
  91.3 1.2 add_bitcast_fusion
  92.6 1.3 collective-permute-start.1
  93.9 15.5 %collective-permute-done.1 = bf16[128,2048]{0,1:T(8,128)(2,1)S(1)} collective-permute-done((bf16[128,2048]{0,1:T(8,128)(2,1)S(1)}, bf16[128,2048]{0,1:T(8,128)(2,1)S(1)}, u32[]{:S(2)}, u32[]{:S(2)}) %collective-permute-start.1) | collective-permute-done | bytes 524320 | tf_op jit(solution)/shard_map/ppermute | solution.py:11
  109.4 1.1 slice_add_fusion
  110.5 1.6 copy.40
  112.1 2.4 fusion.2
  114.5 4.7 %collective-permute-start = (bf16[128,2048]{1,0:T(8,128)(2,1)S(1)}, bf16[128,2048]{1,0:T(8,128)(2,1)S(1)}, u32[]{:S(2)}, u32[]{:S(2)}) collective-permute-start(bf16[128,2048]{1,0:T(8,128)(2,1)S(1)} %get-tuple-element.27), channel_id=1, source_target_pairs={{0,4},{4,8},{8,12},{12,16},{16,20},{20,24},{24,28},{1,5},{5,9},{9,... | collective-permute-start | bytes 1572872 | tf_op jit(solution)/shard_map/ppermute | solution.py:11
  119.2 0.3 copy.37
  119.5 9.7 %collective-permute-done = bf16[128,2048]{1,0:T(8,128)(2,1)S(1)} collective-permute-done((bf16[128,2048]{1,0:T(8,128)(2,1)S(1)}, bf16[128,2048]{1,0:T(8,128)(2,1)S(1)}, u32[]{:S(2)}, u32[]{:S(2)}) %collective-permute-start) | collective-permute-done | bytes 524320 | tf_op jit(solution)/shard_map/ppermute | solution.py:11
  129.2 0.3 copy.36
  129.4 8.1 %fusion.7 = f32[128,16,128]{2,1,0:T(8,128)S(1)} fusion(bf16[1,128,128,16]{1,3,2,0:T(8,128)(2,1)S(1)} %bitcast.49, bf16[1,128,128,16]{1,3,2,0:T(8,128)(2,1)S(1)} %bitcast.52, f32[128,128,256]{2,1,0:T(8,128)} %copy.45), kind=kOutput, calls=%fused_computation.22 | convolution fusion | flops 140509184 | bytes 18874368 | tf_op jit(solution)/shard_map/gts,bsgc->btgc/dot_general | solution.py:37
  137.5 12.9 %convolution_add_fusion = f32[128,16,128]{2,1,0:T(8,128)S(1)} fusion(f32[128,16,128]{2,1,0:T(8,128)S(1)} %fusion.7, bf16[1,128,128,16]{1,3,2,0:T(8,128)(2,1)S(1)} %bitcast.50, bf16[1,128,128,16]{1,3,2,0:T(8,128)(2,1)S(1)} %bitcast.53, f32[128,128,256]{2,1,0:T(8,128)} %copy.45), kind=kOutput, calls=%fused_computation.4 | convolution fusion | flops 153354240 | bytes 19922944 | tf_op jit(solution)/shard_map/gts,bsgc->btgc/dot_general | solution.py:38
  150.4 1.0 fusion.5
  151.5 1.0 copy.43
  152.5 8.6 %fusion.6 = f32[128,128,256]{2,1,0:T(8,128)} fusion(bf16[128,128,16]{0,2,1:T(8,128)(2,1)S(1)} %bitcast.57, bf16[1,128,128,16]{1,3,2,0:T(8,128)(2,1)S(1)} %bitcast.51, bf16[1,128,128,16]{1,3,2,0:T(8,128)(2,1)S(1)} %bitcast.54), kind=kOutput, calls=%fused_computation.21 | convolution fusion | flops 136314880 | bytes 18350080 | tf_op jit(solution)/shard_map/btgc,bsgc->gts/dot_general | solution.py:95
  161.1 17.9 %copy.46 = f32[128,128,256]{0,2,1:T(8,128)} copy(f32[128,128,256]{2,1,0:T(8,128)} %fusion.6) | data formatting | bytes 33554432 | tf_op jit(solution)/shard_map/reshape | solution.py:98
  179.0 13.3 %pad.4 = f32[128,32896]{0,1:T(8,128)} pad(f32[128,32768]{0,1:T(8,128)} %bitcast.48, f32[]{:T(128)} %constant.2.clone.1), padding=0_0x0_128 | pad | bytes 33619972 | tf_op jit(solution)/shard_map/jit(_pad)/pad | solution.py:98
  192.3 17.5 %reshape.67 = f32[128,128,257]{0,2,1:T(8,128)} reshape(f32[128,32896]{0,1:T(8,128)} %pad.4) | data formatting | bytes 33685504 | tf_op jit(solution)/shard_map/reshape | solution.py:99
  209.8 6.7 %reduce_sum.18 = f32[128,257]{0,1:T(8,128)S(1)} reduce(f32[128,128,257]{0,2,1:T(8,128)} %reshape.67, f32[]{:T(128)} %constant.2.clone.1), dimensions={1}, to_apply=%region_1.2 | reduce | flops 4177792 | bytes 16974340 | tf_op jit(solution)/shard_map/reduce_sum | solution.py:99
  216.6 33.0 %all-gather = f32[1024,128]{0,1:T(8,128)S(1)} all-gather(f32[128,128]{0,1:T(8,128)S(1)} %rev.7), channel_id=2, replica_groups=mesh['tok'=8,'wid'=4] {'tok'}, dimensions={0}, use_global_device_ids=true | all-gather | bytes 589824 | tf_op jit(solution)/shard_map/all_gather | solution.py:101
  249.8 0.7 copy.44
  250.5 16.5 %convolution_convert_fusion.1 = bf16[128,2048]{1,0:T(8,128)(2,1)} fusion(bf16[128,8192]{0,1:T(8,128)(2,1)} %all-gather.3.cloned.1.call-done, bf16[8192,2048]{1,0:T(8,128)(2,1)} %param.10), kind=kOutput, calls=%fused_computation.2 | convolution fusion | flops 4295229440 | bytes 36175872 | tf_op jit(solution)/shard_map/dot_general | solution.py:74
  (30 shorter events, 0.9 us)
Async XLA Ops:
  7.2 1.1 copy-start
  7.2 17.8 %copy-start.6 = (f32[128,128]{1,0:T(8,128)S(1)}, f32[128,128]{1,0:T(8,128)}, u32[]{:S(2)}) copy-start(f32[128,128]{1,0:T(8,128)} %param.9) | copy-start | bytes 196612
  7.2 18.1 %copy-start.5 = (bf16[128,2048]{1,0:T(8,128)(2,1)S(1)}, bf16[128,2048]{1,0:T(8,128)(2,1)}, u32[]{:S(2)}) copy-start(bf16[128,2048]{1,0:T(8,128)(2,1)} %param.6) | copy-start | bytes 1572868
  7.2 72.3 %reduce-scatter.2.cloned.1.call-start = ((), (), s32[]{:S(2)}) async-start(), calls=%async_computation.2 | async-start | bytes 2621440 | tf_op jit(solution)/shard_map/reduce_scatter | solution.py:49
  24.9 225.7 %all-gather.3.cloned.1.call-start = ((), (), s32[]{:S(2)}) async-start(), calls=%async_computation.1 | async-start | bytes 2621440 | tf_op jit(solution)/shard_map/all_gather | solution.py:75
  80.7 10.5 %copy-start.2 = (f32[128,128,256]{2,1,0:T(8,128)S(1)}, f32[128,128,256]{2,1,0:T(8,128)}, u32[]{:S(2)}) copy-start(f32[128,128,256]{2,1,0:T(8,128)} %copy.45) | copy-start | bytes 50331652
  91.3 20.8 %copy-start.4 = (bf16[128,2048]{1,0:T(8,128)(2,1)S(1)}, bf16[128,2048]{1,0:T(8,128)(2,1)}, u32[]{:S(2)}) copy-start(bf16[128,2048]{1,0:T(8,128)(2,1)} %param.7) | copy-start | bytes 1572868
  92.6 16.8 %collective-permute-start.1 = (bf16[128,2048]{0,1:T(8,128)(2,1)S(1)}, bf16[128,2048]{0,1:T(8,128)(2,1)S(1)}, u32[]{:S(2)}, u32[]{:S(2)}) collective-permute-start(bf16[128,2048]{0,1:T(8,128)(2,1)S(1)} %bitcast.61), channel_id=1, source_target_pairs={{4,0},{8,4},{12,8},{16,12},{20,16},{24,20},{28,24},{5,1},{9,5},{13... | collective-permute-start | bytes 1572872 | tf_op jit(solution)/shard_map/ppermute | solution.py:11
  114.5 14.7 %collective-permute-start = (bf16[128,2048]{1,0:T(8,128)(2,1)S(1)}, bf16[128,2048]{1,0:T(8,128)(2,1)S(1)}, u32[]{:S(2)}, u32[]{:S(2)}) collective-permute-start(bf16[128,2048]{1,0:T(8,128)(2,1)S(1)} %get-tuple-element.27), channel_id=1, source_target_pairs={{0,4},{4,8},{8,12},{12,16},{16,20},{20,24},{24,28},{1,5},{5,9},{9,... | collective-permute-start | bytes 1572872 | tf_op jit(solution)/shard_map/ppermute | solution.py:11
  137.5 12.9 %copy-start.3 = (bf16[2048,128]{1,0:T(8,128)(2,1)S(1)}, bf16[2048,128]{1,0:T(8,128)(2,1)}, u32[]{:S(2)}) copy-start(bf16[2048,128]{1,0:T(8,128)(2,1)} %reduce-scatter.2.cloned.1.call-done) | copy-start | bytes 1572868
  250.5 16.6 %copy-start.1 = (bf16[128,2048]{1,0:T(8,128)(2,1)S(1)}, bf16[128,2048]{1,0:T(8,128)(2,1)}, u32[]{:S(2)}) copy-start(bf16[128,2048]{1,0:T(8,128)(2,1)} %param.11) | copy-start | bytes 1572868
Sparse Core Ops, SparseCore 0:
  25.0 34.1 reduce-scatter.1
  151.6 23.7 all-gather.2
